TPU v7x, 32 devices: a whole 2x2x4 slice. The times are simulated.
32 devices in a mesh: groups: 2 (over x), tok: 16 (over z, y, core).
Axes of the slice: x: 2, y: 2, z: 4, core: 2. Of those that a mesh axis runs over, the one named last changes fastest.
Arguments:
- single: bfloat16 [512, 8, 768], P(('groups', 'tok')), parts along dimension 0, may hold values from -6 to 6
- pair: bfloat16 [512, 256, 128], P(('groups', 'tok')), parts along dimension 0, may hold values from -400 to 400, as said below
- chain: int32 [512], P(('groups', 'tok')), parts along dimension 0, may hold values from 0 to 7, never falling along the last dimension, each value on 1 to 64 neighbouring positions
- residue: int32 [512], P(('groups', 'tok')), parts along dimension 0, may hold values from 0 to 510, as said below
- valid: int32 [512], P(('groups', 'tok')), parts along dimension 0, may hold values 0 or 1
- w_query: bfloat16 [768, 768], replicated, may hold values from -0.21875 to 0.21875
- w_key: bfloat16 [768, 768], replicated, may hold values from -0.21875 to 0.21875
- w_value: bfloat16 [768, 768], replicated, may hold values from -0.21875 to 0.21875
- w_gate: bfloat16 [768, 768], replicated, may hold values from -0.21875 to 0.21875
- w_out: bfloat16 [768, 768], replicated, may hold values from -0.21875 to 0.21875
- w_pair: bfloat16 [128, 16], replicated, may hold values from -1.1953125 to 1.1953125
- rel_table: float32 [66, 16], replicated, may hold values from -6 to 6
Outputs:
- updated: bfloat16 [512, 8, 768], P(('groups', 'tok')), parts along dimension 0
There are 2 independent parts, one for each index of `groups`. A program takes and returns all parts, laid end to end along the dimension named above; an argument that names none is the same for every part. Nothing has to cross between parts.
Inputs may be any that keep to these rules, and one draw needn't show every extreme that they name: `pair`: pair entries are of order one, except possibly in a few query rows where two entries have many times the usual size. `residue`: starts at 0 and rises from each token to the next, by 1 or 2 except into the last token, which holds the largest value.
All inputs are finite; a program needn't handle non-finite values. No bound on the sum of `valid` on one device may be relied on, other than what follows from the above.
Results may differ from a plain program's by a relative error of at most 0.0045.
Values may be sent and summed in bfloat16 or wider, within the bound.
A program may use at most 128 MiB of HBM per device.

v0:
```python
import math

import jax
import jax.numpy as jnp
from jax import lax
from jax.sharding import PartitionSpec as P

NORM_EPS = 1e-05
MASK_PENALTY = 10000.0


def layer_normed(values_in):
    mean_val = jnp.mean(values_in, axis=-1, keepdims=True)
    centred = values_in - mean_val
    spread = jnp.mean(centred * centred, axis=-1, keepdims=True)
    return centred * lax.rsqrt(spread + NORM_EPS)


def shards(
    single, pair, chain, residue, valid, w_query, w_key, w_value, w_gate, w_out, w_pair, rel_table
):
    local_tokens, sample_count, width = single.shape
    head_count = w_pair.shape[1]
    head_size = width // head_count
    total_keys = pair.shape[1]
    channels = pair.shape[2]
    rel_bins = rel_table.shape[0]
    rel_reach = (rel_bins - 2) // 2
    scale_factor = 1.0 / math.sqrt(head_size)
    bucket_ids = jnp.arange(rel_bins, dtype=jnp.int32)
    normed = layer_normed(single.astype(jnp.float32)).astype(jnp.bfloat16)
    flat_rows = normed.reshape(local_tokens * sample_count, width)

    def project(weight):
        return jnp.dot(flat_rows, weight, preferred_element_type=jnp.float32)

    query_proj = (
        project(w_query)
        .astype(jnp.bfloat16)
        .reshape(local_tokens, sample_count, head_count, head_size)
    )
    key_proj = project(w_key).astype(jnp.bfloat16).reshape(local_tokens, sample_count, width)
    value_proj = project(w_value).astype(jnp.bfloat16).reshape(local_tokens, sample_count, width)
    gate_proj = jax.nn.sigmoid(project(w_gate)).reshape(
        local_tokens, sample_count, head_count, head_size
    )
    bias_rows = jnp.dot(
        pair.reshape(local_tokens * total_keys, channels),
        w_pair,
        preferred_element_type=jnp.float32,
    ).reshape(local_tokens, total_keys, head_count)
    token_axis = lax.axis_size("tok")
    quarters = token_axis // head_count
    quarter_rows = local_tokens // quarters
    my_index = lax.axis_index("tok")
    my_quarter = my_index // head_count
    my_head = my_index % head_count
    query_split = query_proj.reshape(quarters, quarter_rows, sample_count, head_count, head_size)
    query_send = jnp.transpose(query_split, (0, 3, 1, 2, 4)).reshape(
        token_axis, quarter_rows, sample_count * head_size
    )
    both_heads = jnp.stack(
        [
            key_proj.reshape(local_tokens, sample_count, head_count, head_size),
            value_proj.reshape(local_tokens, sample_count, head_count, head_size),
        ],
        axis=3,
    )
    both_heads = jnp.transpose(both_heads, (2, 0, 1, 3, 4))
    kv_send = jnp.broadcast_to(both_heads[None], (quarters,) + both_heads.shape).reshape(
        token_axis, local_tokens, sample_count * 2 * head_size
    )
    query_got, kv_got = (
        lax.all_to_all(query_send, "tok", split_axis=0, concat_axis=1, tiled=True),
        lax.all_to_all(kv_send, "tok", split_axis=0, concat_axis=1, tiled=True),
    )
    bias_send = jnp.transpose(
        bias_rows.reshape(quarters, quarter_rows, total_keys, head_count), (0, 3, 1, 2)
    ).reshape(token_axis, quarter_rows, total_keys)
    meta_one = jnp.stack([chain, residue, valid], axis=0).astype(jnp.float32)
    meta_send = jnp.broadcast_to(meta_one[None], (token_axis, 3, local_tokens))
    bias_got, meta_got = (
        lax.all_to_all(bias_send, "tok", split_axis=0, concat_axis=1, tiled=True),
        lax.all_to_all(meta_send, "tok", split_axis=0, concat_axis=1, tiled=True),
    )
    query_rows = token_axis * quarter_rows
    query_all = query_got.reshape(query_rows, sample_count, head_size)
    kv_all = kv_got.reshape(total_keys, sample_count, 2, head_size)
    key_all = kv_all[:, :, 0]
    value_all = kv_all[:, :, 1]
    bias_all = bias_got.reshape(query_rows, total_keys)
    meta_int = jnp.transpose(meta_got.reshape(token_axis, 3, local_tokens), (1, 0, 2)).astype(
        jnp.int32
    )
    chain_keys = meta_int[0].reshape(total_keys)
    residue_keys = meta_int[1].reshape(total_keys)
    valid_keys = meta_int[2].reshape(total_keys)
    chain_query = lax.dynamic_slice_in_dim(
        meta_int[0].reshape(token_axis, quarters, quarter_rows), my_quarter, 1, 1
    ).reshape(query_rows)
    residue_query = lax.dynamic_slice_in_dim(
        meta_int[1].reshape(token_axis, quarters, quarter_rows), my_quarter, 1, 1
    ).reshape(query_rows)
    rel_column = lax.dynamic_slice_in_dim(rel_table, my_head, 1, 1)
    mask_keys = (valid_keys.astype(jnp.float32) - 1.0) * MASK_PENALTY
    block_rows = math.gcd(query_rows, 64)

    def head_block(block_index):
        start_row = block_index * block_rows
        query_block = lax.dynamic_slice_in_dim(query_all, start_row, block_rows, 0)
        bias_block = lax.dynamic_slice_in_dim(bias_all, start_row, block_rows, 0)
        chain_block = lax.dynamic_slice_in_dim(chain_query, start_row, block_rows, 0)
        residue_block = lax.dynamic_slice_in_dim(residue_query, start_row, block_rows, 0)
        same_chain = chain_block[:, None] == chain_keys[None, :]
        offset = (
            jnp.clip(residue_block[:, None] - residue_keys[None, :], -rel_reach, rel_reach)
            + rel_reach
        )
        bucket = jnp.where(same_chain, offset, rel_bins - 1)
        one_hot = (bucket[:, :, None] == bucket_ids).astype(jnp.float32)
        rel_bias = jnp.einsum("qkb,bh->qkh", one_hot, rel_column, precision=lax.Precision.HIGHEST)[
            :, :, 0
        ]
        total_bias = bias_block + rel_bias + mask_keys[None, :]
        scores = (
            jnp.einsum("qsd,ksd->sqk", query_block, key_all, preferred_element_type=jnp.float32)
            * scale_factor
            + total_bias[None]
        )
        top_score = jnp.max(scores, axis=-1, keepdims=True)
        probs = jnp.exp(scores - top_score)
        mass = jnp.sum(probs, axis=-1)
        weighted = jnp.einsum(
            "sqk,ksd->sqd",
            probs.astype(jnp.bfloat16),
            value_all,
            preferred_element_type=jnp.float32,
        )
        return jnp.transpose(weighted / mass[..., None], (1, 0, 2))

    attended_rows = lax.map(head_block, jnp.arange(query_rows // block_rows, dtype=jnp.int32))
    result_send = attended_rows.reshape(token_axis, quarter_rows, sample_count * head_size)
    result_got = lax.all_to_all(
        result_send.astype(jnp.bfloat16), "tok", split_axis=0, concat_axis=1, tiled=True
    ).astype(result_send.dtype)
    attended = jnp.transpose(
        result_got.reshape(quarters, head_count, quarter_rows, sample_count, head_size),
        (0, 2, 3, 1, 4),
    ).reshape(local_tokens, sample_count, head_count, head_size)
    gated = (gate_proj * attended).reshape(local_tokens * sample_count, width).astype(jnp.bfloat16)
    out_rows = jnp.dot(gated, w_out, preferred_element_type=jnp.float32).reshape(
        local_tokens, sample_count, width
    )
    return (single.astype(jnp.float32) + out_rows).astype(jnp.bfloat16)


def solution(mesh):
    placed = (
        P(("groups", "tok"), None, None),
        P(("groups", "tok"), None, None),
        P(("groups", "tok")),
        P(("groups", "tok")),
        P(("groups", "tok")),
        P(),
        P(),
        P(),
        P(),
        P(),
        P(),
        P(),
    )
    return jax.shard_map(
        shards,
        mesh=mesh,
        in_specs=placed,
        out_specs=P(("groups", "tok"), None, None),
        check_vma=False,
    )
```

profile of v0, /device:TPU:0, one launch (start us, length us, event | category | flops | bytes accessed | tf_op | source)
XLA Modules:
  0.0 108.9 jit_solution(10050591456605176731)
XLA Ops:
  0.0 0.8 add_convert_fusion
  0.8 0.6 broadcast_in_dim.12
  1.4 7.4 %all-to-all-start.3 = ((f32[16,3,16]{2,1,0:T(4,128)}), f32[16,3,16]{2,1,0:T(4,128)S(1)}, u32[]{:S(2)}, u32[]{:S(2)}) async-start(f32[16,3,16]{2,1,0:T(4,128)} %broadcast_in_dim.12), calls=%async_computation.3 | async-start | bytes 65536 | tf_op jit(solution)/shard_map/all_to_all | solution.py:84
  8.8 1.1 %convert_reduce_fusion = f32[16,8]{1,0:T(8,128)S(1)} fusion(bf16[16,8,768]{2,1,0:T(8,128)(2,1)} %param.14), kind=kLoop, calls=%fused_computation.36 | loop fusion | flops 196480 | bytes 197120 | tf_op jit(solution)/shard_map/reduce_sum | solution.py:13
  10.0 1.1 %fusion.28 = f32[16,8]{1,0:T(8,128)S(1)} fusion(bf16[16,8,768]{2,1,0:T(8,128)(2,1)} %param.14, f32[16,8]{1,0:T(8,128)S(1)} %broadcast_multiply_fusion), kind=kLoop, calls=%fused_computation.40 | loop fusion | flops 393088 | bytes 197632 | tf_op jit(solution)/shard_map/reduce_sum | solution.py:15
  11.1 1.3 %convolution_convert_fusion.1 = bf16[128,768]{1,0:T(8,128)(2,1)S(1)} fusion(bf16[768,768]{1,0:T(8,128)(2,1)S(1)} %copy-done, bf16[16,8,768]{2,1,0:T(8,128)(2,1)} %param.14, f32[16,8]{1,0:T(8,128)S(1)} %add_rsqrt_fusion, f32[16,8]{1,0:T(8,128)S(1)} %broadcast_multiply_fusion), kind=kOutput, calls=%fused_computation.30 | convolution fusion | flops 151486464 | bytes 1573888 | tf_op jit(solution)/shard_map/dot_general | solution.py:35
  12.8 0.6 stack_reshape_reshape.6
  13.5 1.0 copy.43
  14.5 0.6 reshape_reshape.4
  15.3 1.0 reshape.199
  16.3 6.0 %all-to-all-start = ((bf16[16,16,384]{2,1,0:T(8,128)(2,1)}), bf16[16,16,384]{2,1,0:T(8,128)(2,1)}, u32[]{:S(2)}, u32[]{:S(2)}) async-start(bf16[16,16,384]{2,1,0:T(8,128)(2,1)} %reshape.199), calls=%async_computation | async-start | bytes 393216 | tf_op jit(solution)/shard_map/all_to_all | solution.py:74
  22.4 1.6 %convolution_convert_fusion = bf16[128,768]{1,0:T(8,128)(2,1)S(1)} fusion(bf16[768,768]{1,0:T(8,128)(2,1)} %param.21, bf16[16,8,768]{2,1,0:T(8,128)(2,1)S(1)} %copy-done.1, f32[16,8]{1,0:T(8,128)S(1)} %add_rsqrt_fusion, f32[16,8]{1,0:T(8,128)S(1)} %broadcast_multiply_fusion), kind=kOutput, calls=%fused_computation.29 | convolution fusion | flops 151486464 | bytes 1573888 | tf_op jit(solution)/shard_map/dot_general | solution.py:35
  24.0 0.6 stack_reshape_reshape.7
  24.7 1.0 copy.44
  25.7 2.8 %maximum_bitcast_fusion = bf16[16,16,8,2,48]{4,3,2,1,0:T(2,128)(2,1)S(1)} fusion(bf16[16,8,16,1,48]{4,3,1,0,2:T(2,128)(2,1)S(1)} %copy.44, bf16[16,8,16,1,48]{4,3,1,0,2:T(2,128)(2,1)S(1)} %copy.43), kind=kLoop, calls=%fused_computation.34 | loop fusion | flops 786432 | bytes 786432 | tf_op jit(solution)/shard_map/transpose | solution.py:69
  28.5 2.0 %reshape_broadcast_in_dim.3 = bf16[16,16,768]{2,1,0:T(8,128)(2,1)} reshape(bf16[16,16,8,2,48]{4,3,2,1,0:T(2,128)(2,1)S(1)} %maximum_bitcast_fusion) | data formatting | bytes 786432 | tf_op jit(solution)/shard_map/reshape;broadcast_in_dim | solution.py:70
  30.5 1.0 all-to-all-done
  31.4 5.0 %all-to-all-start.1 = ((bf16[16,16,768]{2,1,0:T(8,128)(2,1)}), bf16[16,16,768]{2,1,0:T(8,128)(2,1)S(1)}, u32[]{:S(2)}, u32[]{:S(2)}) async-start(bf16[16,16,768]{2,1,0:T(8,128)(2,1)} %reshape_broadcast_in_dim.3), calls=%async_computation.1 | async-start | bytes 786432 | tf_op jit(solution)/shard_map/all_to_all | solution.py:75
  36.8 0.9 copy.46
  37.7 0.7 constant_dynamic-slice_fusion
  38.8 9.8 %all-to-all-done.1 = bf16[16,16,768]{2,1,0:T(8,128)(2,1)S(1)} async-done(((bf16[16,16,768]{2,1,0:T(8,128)(2,1)}), bf16[16,16,768]{2,1,0:T(8,128)(2,1)S(1)}, u32[]{:S(2)}, u32[]{:S(2)}) %all-to-all-start.1) | async-done | bytes 393248 | tf_op jit(solution)/shard_map/all_to_all | solution.py:75
  48.6 4.4 %all-to-all-start.2 = ((f32[16,16,256]{2,1,0:T(8,128)}), f32[16,16,256]{2,1,0:T(8,128)}, u32[]{:S(2)}, u32[]{:S(2)}) async-start(f32[16,16,256]{2,1,0:T(8,128)} %copy.46), calls=%async_computation.2 | async-start | bytes 524288 | tf_op jit(solution)/shard_map/all_to_all | solution.py:83
  53.1 1.4 %reshape.200 = bf16[256,8,48]{2,1,0:T(8,128)(2,1)S(1)} reshape(bf16[16,16,384]{2,1,0:T(8,128)(2,1)} %all-to-all-done) | data formatting | bytes 393216 | tf_op jit(solution)/shard_map/reshape | solution.py:87
  54.5 1.0 copy.48
  55.5 1.2 %reshape.201 = bf16[256,8,2,48]{3,2,1,0:T(2,128)(2,1)S(1)} reshape(bf16[16,16,768]{2,1,0:T(8,128)(2,1)S(1)} %all-to-all-done.1) | data formatting | bytes 786432 | tf_op jit(solution)/shard_map/reshape | solution.py:88
  56.8 2.3 %fusion.43 = (bf16[256,8,1,48]{3,2,1,0:T(2,128)(2,1)}, bf16[256,8,1,48]{3,2,1,0:T(2,128)(2,1)S(1)}) fusion(bf16[256,8,2,48]{3,2,1,0:T(2,128)(2,1)S(1)} %reshape.201), kind=kLoop, calls=%fused_computation.58 | loop fusion | bytes 786432 | tf_op jit(solution)/shard_map/slice | solution.py:90
  59.1 3.4 %copy.47 = bf16[256,8,1,48]{0,3,2,1:T(8,128)(2,1)} copy(bf16[256,8,1,48]{3,2,1,0:T(2,128)(2,1)} %get-tuple-element.188) | data formatting | bytes 393216 | tf_op jit(solution)/shard_map/slice | solution.py:90
  62.5 0.8 copy.45
  63.3 25.9 %while.12 = (s32[]{:T(128)}, bf16[4,64,8,48]{1,3,2,0:T(8,128)(2,1)S(1)}, s32[4]{0:T(128)S(1)}, bf16[256,8,48]{0,2,1:T(8,128)(2,1)S(1)}, bf16[256,8,48]{0,2,1:T(8...) while((s32[]{:T(128)}, ...), condition=%wide.wide.region_5.6_spmd.clone, body=%wide.wide.region_2.5_spmd.clone.sunk | while | flops 40279044 | bytes 5688351 | solution.py:141
  63.3 0.6 dynamic_slice.45
  64.8 0.6 iota_compare_fusion.3
  65.5 2.4 %fusion.76 = f32[1,64,256]{2,0,1:T(1,128)S(1)} fusion(pred[64,256,66]{1,0,2:T(32,128)(4,1)S(1)} %iota_compare_fusion.3, f32[66,1]{0,1:T(1,128)S(1)} %get-tuple-element.388), kind=kOutput, calls=%fused_computation.1.clone.clone.1 | convolution fusion | flops 12976128 | bytes 1147144 | tf_op jit(solution)/shard_map/while/body/eval_jaxpr/qkb,bh->qkh/dot_general | solution.py:121
  67.8 0.9 fusion.77
  69.8 0.6 dynamic_slice.45
  71.3 0.6 iota_compare_fusion.3
  72.0 2.4 %fusion.76 = f32[1,64,256]{2,0,1:T(1,128)S(1)} fusion(pred[64,256,66]{1,0,2:T(32,128)(4,1)S(1)} %iota_compare_fusion.3, f32[66,1]{0,1:T(1,128)S(1)} %get-tuple-element.388), kind=kOutput, calls=%fused_computation.1.clone.clone.1 | convolution fusion | flops 12976128 | bytes 1147144 | tf_op jit(solution)/shard_map/while/body/eval_jaxpr/qkb,bh->qkh/dot_general | solution.py:121
  74.3 0.9 fusion.77
  76.3 0.6 dynamic_slice.45
  77.8 0.6 iota_compare_fusion.3
  78.4 2.4 %fusion.76 = f32[1,64,256]{2,0,1:T(1,128)S(1)} fusion(pred[64,256,66]{1,0,2:T(32,128)(4,1)S(1)} %iota_compare_fusion.3, f32[66,1]{0,1:T(1,128)S(1)} %get-tuple-element.388), kind=kOutput, calls=%fused_computation.1.clone.clone.1 | convolution fusion | flops 12976128 | bytes 1147144 | tf_op jit(solution)/shard_map/while/body/eval_jaxpr/qkb,bh->qkh/dot_general | solution.py:121
  80.8 0.9 fusion.77
  82.8 0.6 dynamic_slice.45
  84.3 0.6 iota_compare_fusion.3
  84.9 2.4 %fusion.76 = f32[1,64,256]{2,0,1:T(1,128)S(1)} fusion(pred[64,256,66]{1,0,2:T(32,128)(4,1)S(1)} %iota_compare_fusion.3, f32[66,1]{0,1:T(1,128)S(1)} %get-tuple-element.388), kind=kOutput, calls=%fused_computation.1.clone.clone.1 | convolution fusion | flops 12976128 | bytes 1147144 | tf_op jit(solution)/shard_map/while/body/eval_jaxpr/qkb,bh->qkh/dot_general | solution.py:121
  87.3 0.9 fusion.77
  90.0 14.5 %all_to_all.20 = bf16[16,16,384]{2,1,0:T(8,128)(2,1)S(1)} all-to-all(bf16[16,16,384]{2,1,0:T(8,128)(2,1)S(1)} %convert_element_type.72), channel_id=1, replica_groups=mesh['groups'=2,'tok'=16] {'tok'}, dimensions={0} | all-to-all | bytes 393216 | tf_op jit(solution)/shard_map/all_to_all | solution.py:143
  104.9 0.6 copy.52
  106.0 3.0 %fusion.22 = bf16[16,8,768]{2,1,0:T(8,128)(2,1)} fusion(bf16[768,768]{1,0:T(8,128)(2,1)} %param.23, f32[128,768]{1,0:T(8,128)S(1)} %reshape.209, bf16[768,768]{1,0:T(8,128)(2,1)} %param.22, bf16[16,8,768]{2,1,0:T(8,128)(2,1)S(1)} %copy-done.1, f32[16,8]{1,0:T(8,128)S(1)} %add_rsqrt_fusion, f32[16,8]{1,0:T(8,128)S(1)} %broadcast_multiply_fusion), kind=kOutput, calls=%fused_computation.28 | convolution fusion | flops 303169536 | bytes 3146752 | tf_op jit(solution)/shard_map/dot_general | solution.py:151
  (71 shorter events, 8.1 us)
Async XLA Ops:
  0.0 11.1 %copy-start = (bf16[768,768]{1,0:T(8,128)(2,1)S(1)}, bf16[768,768]{1,0:T(8,128)(2,1)}, u32[]{:S(2)}) copy-start(bf16[768,768]{1,0:T(8,128)(2,1)} %param.20) | copy-start | bytes 3538948
  0.0 12.4 %copy-start.1 = (bf16[16,8,768]{2,1,0:T(8,128)(2,1)S(1)}, bf16[16,8,768]{2,1,0:T(8,128)(2,1)}, u32[]{:S(2)}) copy-start(bf16[16,8,768]{2,1,0:T(8,128)(2,1)} %param.14) | copy-start | bytes 589828
  1.4 14.9 %all-to-all-start.3 = ((f32[16,3,16]{2,1,0:T(4,128)}), f32[16,3,16]{2,1,0:T(4,128)S(1)}, u32[]{:S(2)}, u32[]{:S(2)}) async-start(f32[16,3,16]{2,1,0:T(4,128)} %broadcast_in_dim.12), calls=%async_computation.3 | async-start | bytes 65536 | tf_op jit(solution)/shard_map/all_to_all | solution.py:84
  8.8 3.6 %copy-start.3 = (bf16[768,768]{1,0:T(8,128)(2,1)S(1)}, bf16[768,768]{1,0:T(8,128)(2,1)}, u32[]{:S(2)}) copy-start(bf16[768,768]{1,0:T(8,128)(2,1)} %param.19) | copy-start | bytes 3538948
  16.3 15.1 %all-to-all-start = ((bf16[16,16,384]{2,1,0:T(8,128)(2,1)}), bf16[16,16,384]{2,1,0:T(8,128)(2,1)}, u32[]{:S(2)}, u32[]{:S(2)}) async-start(bf16[16,16,384]{2,1,0:T(8,128)(2,1)} %reshape.199), calls=%async_computation | async-start | bytes 393216 | tf_op jit(solution)/shard_map/all_to_all | solution.py:74
  28.5 8.0 %copy-start.4 = (bf16[16,256,128]{2,1,0:T(8,128)(2,1)S(1)}, bf16[16,256,128]{2,1,0:T(8,128)(2,1)}, u32[]{:S(2)}) copy-start(bf16[16,256,128]{2,1,0:T(8,128)(2,1)} %param.15) | copy-start | bytes 3145732
  28.5 8.0 %copy-start.9 = (bf16[128,16]{0,1:T(8,128)(2,1)S(1)}, bf16[128,16]{0,1:T(8,128)(2,1)}, u32[]{:S(2)}) copy-start(bf16[128,16]{0,1:T(8,128)(2,1)} %param.24) | copy-start | bytes 12292
  31.4 17.2 %all-to-all-start.1 = ((bf16[16,16,768]{2,1,0:T(8,128)(2,1)}), bf16[16,16,768]{2,1,0:T(8,128)(2,1)S(1)}, u32[]{:S(2)}, u32[]{:S(2)}) async-start(bf16[16,16,768]{2,1,0:T(8,128)(2,1)} %reshape_broadcast_in_dim.3), calls=%async_computation.1 | async-start | bytes 786432 | tf_op jit(solution)/shard_map/all_to_all | solution.py:75
  38.5 18.3 %copy-start.7 = (s32[1,16,16]{2,0,1:T(1,128)}, s32[1,16,16]{2,0,1:T(1,128)S(1)}, u32[]{:S(2)}) copy-start(s32[1,16,16]{2,0,1:T(1,128)S(1)} %get-tuple-element.190) | copy-start | bytes 3076
  38.5 18.3 %copy-start.8 = (s32[1,16,16]{2,0,1:T(1,128)}, s32[1,16,16]{2,0,1:T(1,128)S(1)}, u32[]{:S(2)}) copy-start(s32[1,16,16]{2,0,1:T(1,128)S(1)} %get-tuple-element.191) | copy-start | bytes 3076
  48.6 14.6 %all-to-all-start.2 = ((f32[16,16,256]{2,1,0:T(8,128)}), f32[16,16,256]{2,1,0:T(8,128)}, u32[]{:S(2)}, u32[]{:S(2)}) async-start(f32[16,16,256]{2,1,0:T(8,128)} %copy.46), calls=%async_computation.2 | async-start | bytes 524288 | tf_op jit(solution)/shard_map/all_to_all | solution.py:83
  59.0 4.3 %copy-start.2 = (bf16[256,8,48]{0,2,1:T(8,128)(2,1)S(1)}, bf16[256,8,48]{0,2,1:T(8,128)(2,1)}, u32[]{:S(2)}) copy-start(bf16[256,8,48]{0,2,1:T(8,128)(2,1)} %copy.48) | copy-start | bytes 589828
  59.0 4.3 %copy-start.5 = (bf16[4,64,8,48]{1,3,2,0:T(8,128)(2,1)S(1)}, bf16[4,64,8,48]{1,3,2,0:T(8,128)(2,1)}, u32[]{:S(2)}) copy-start(bf16[4,64,8,48]{1,3,2,0:T(8,128)(2,1)} %custom-call) | copy-start | bytes 589828
  67.8 1.7 %copy-start.6 = (bf16[256,8,48]{0,2,1:T(8,128)(2,1)S(1)}, bf16[256,8,48]{0,2,1:T(8,128)(2,1)}, u32[]{:S(2)}) copy-start(bf16[256,8,48]{0,2,1:T(8,128)(2,1)} %get-tuple-element.390) | copy-start | bytes 589828 | tf_op jit(solution)/shard_map/while
  74.3 1.7 %copy-start.6 = (bf16[256,8,48]{0,2,1:T(8,128)(2,1)S(1)}, bf16[256,8,48]{0,2,1:T(8,128)(2,1)}, u32[]{:S(2)}) copy-start(bf16[256,8,48]{0,2,1:T(8,128)(2,1)} %get-tuple-element.390) | copy-start | bytes 589828 | tf_op jit(solution)/shard_map/while
  80.8 1.7 %copy-start.6 = (bf16[256,8,48]{0,2,1:T(8,128)(2,1)S(1)}, bf16[256,8,48]{0,2,1:T(8,128)(2,1)}, u32[]{:S(2)}) copy-start(bf16[256,8,48]{0,2,1:T(8,128)(2,1)} %get-tuple-element.390) | copy-start | bytes 589828 | tf_op jit(solution)/shard_map/while
  87.3 1.7 %copy-start.6 = (bf16[256,8,48]{0,2,1:T(8,128)(2,1)S(1)}, bf16[256,8,48]{0,2,1:T(8,128)(2,1)}, u32[]{:S(2)}) copy-start(bf16[256,8,48]{0,2,1:T(8,128)(2,1)} %get-tuple-element.390) | copy-start | bytes 589828 | tf_op jit(solution)/shard_map/while
where the time goes:
time: 110 us; the launch traced here: 109 us
  local copies, waits for them, and re-layouts  24.9 us (23%)
  starting transfers between devices  22.8 us (21%)
  matrix products  19.2 us (17%)
  blocking collectives  14.5 us (13%)
  other arithmetic  13.5 us (12%)
  waiting for transfers between devices  10.8 us (10%)
  loops' own time  2.86 us (3%)
    all_to_all x1, blocking collectives, shards(): lax.all_to_all(result_send.astype(jnp.bfloat16), 'tok', split_axis=0, con...  14.5 us
    all_to_all x1, waiting for transfers between devices, shards(): lax.all_to_all(kv_send, 'tok', split_axis=0, concat_axis=1, tiled=True)  9.84 us
    dot_general x4, matrix products, head_block(): jnp.einsum('qkb,bh->qkh', one_hot, rel_column, precision=lax.Precision.HI...  9.43 us
    all_to_all x1, starting transfers between devices, shards(): lax.all_to_all(meta_send, 'tok', split_axis=0, concat_axis=1, tiled=True)  7.39 us
    all_to_all x1, starting transfers between devices, shards(): lax.all_to_all(query_send, 'tok', split_axis=0, concat_axis=1, tiled=True)  6.05 us
    slice x2, local copies, waits for them, and re-layouts, shards(): value_all = kv_all[:, :, 1]  5.7 us
    all_to_all x1, starting transfers between devices, shards(): lax.all_to_all(kv_send, 'tok', split_axis=0, concat_axis=1, tiled=True)  5 us
    all_to_all x1, starting transfers between devices, shards(): lax.all_to_all(bias_send, 'tok', split_axis=0, concat_axis=1, tiled=True)  4.37 us
  transfers between devices with their start and end apart: 4, of which 2 were waited for; matrix products, arithmetic and copies ran while one was open for 26% of the time, Pallas kernels for 0%

commit v1 on v0

v1 whole, which is shorter than its diff:
```python
import functools
import math

import jax
import jax.numpy as jnp
from jax import lax
from jax.experimental import pallas as pl
from jax.experimental.pallas import tpu as pltpu
from jax.sharding import PartitionSpec as P

NORM_EPS = 1e-05
MASK_PENALTY = 10000.0
F32 = jnp.float32
BF16 = jnp.bfloat16
NT = (((1,), (1,)), ((), ()))


def normed_rows(x):
    x = x.astype(F32)
    mean = jnp.mean(x, axis=-1, keepdims=True)
    centred = x - mean
    spread = jnp.mean(centred * centred, axis=-1, keepdims=True)
    return (centred * lax.rsqrt(spread + NORM_EPS)).astype(BF16)


def kernel(
    n, ny, x_ref, meta_ref, chain_ref, residue_ref, pair_ref, wq_ref, wk_ref, wv_ref, wg_ref, wo_ref,
    wp_ref, rel_ref, out_ref,
    buf, meta_buf, mask_buf, bias_buf, q_buf, gate_buf, gated_buf,
    meta_send, meta_recv, recv, send_z, send_y, send_c,
):
    units, per, rows, width = x_ref.shape
    heads = wp_ref.shape[0]
    head_size = width // heads
    keys = n * rows
    rel_bins = rel_ref.shape[1]
    reach = (rel_bins - 2) // 2
    scale = 1.0 / math.sqrt(head_size)
    nz = n // (2 * ny)
    phases = units // 2
    me = lax.axis_index("tok")
    c = me % 2
    y = (me // 2) % ny
    z = me // (2 * ny)
    partner = me + 1 - 2 * c
    across = (z * ny + (y + 1) % ny) * 2 + c

    def place(zz, yy, cc):
        return (zz * ny + yy) * 2 + cc

    def copy(src, dst, ssem, rsem, to):
        return pltpu.make_async_remote_copy(
            src_ref=src, dst_ref=dst, send_sem=ssem, recv_sem=rsem,
            device_id={"tok": to}, device_id_type=pl.DeviceIdType.MESH,
        )

    barrier = pltpu.get_barrier_semaphore()

    @pl.loop(1, n)
    def _(k):
        pl.semaphore_signal(
            barrier, inc=1, device_id={"tok": (me + k) % n}, device_id_type=pl.DeviceIdType.MESH
        )

    pl.semaphore_wait(barrier, n - 1)

    def first_copy(p, k):
        g = k % 2
        zz = (z + k // 2) % nz
        to = place(zz, y, (c + g) % 2)
        u = 2 * p + (c + g) % 2
        return copy(x_ref.at[u], buf.at[u, me], send_z.at[p, k], recv.at[u, me], to)

    def own_across(p):
        u = 2 * p + c
        return copy(x_ref.at[u], buf.at[u, me], send_y.at[p, 0], recv.at[u, me], across)

    def own_partner(p):
        u = 2 * p + c
        return copy(x_ref.at[u], buf.at[u, me], send_c.at[p, 0], recv.at[u, me], partner)

    def source(k):
        return place((z + k // 2) % nz, y, (c + k) % 2)

    def source_across(k):
        return place((z + k // 2) % nz, (y + 1) % ny, (c + k) % 2)

    def forward_across(p, k):
        u = 2 * p + c
        j = source(k)
        return copy(buf.at[u, j], buf.at[u, j], send_y.at[p, k], recv.at[u, j], across)

    def forward_partner(p, k):
        u = 2 * p + c
        j = source(k)
        return copy(buf.at[u, j], buf.at[u, j], send_c.at[p, k], recv.at[u, j], partner)

    def forward_partner_across(p, k):
        u = 2 * p + c
        j = source_across(k)
        return copy(
            buf.at[u, j], buf.at[u, j], send_c.at[p, 2 * nz + k], recv.at[u, j], partner
        )

    def wait_unit(u, j):
        copy(buf.at[u, j], buf.at[u, j], send_c.at[0, 0], recv.at[u, j], partner).wait_recv()

    def start_phase(p):
        own_across(p).start()

        @pl.loop(1, 2 * nz)
        def _(k):
            first_copy(p, k).start()

        own_partner(p).start()

    def pass_on(p):
        @pl.loop(1, 2 * nz)
        def _(k):
            wait_unit(2 * p + c, source(k))
            forward_across(p, k).start()

            @pl.when(k != 1)
            def _():
                forward_partner(p, k).start()

    def pass_back(p):
        @pl.loop(0, 2 * nz)
        def _(k):
            wait_unit(2 * p + c, source_across(k))
            forward_partner_across(p, k).start()

    def finish_phase(p):
        @pl.loop(1, n)
        def _(k):
            wait_unit(2 * p + 1 - c, (me + k) % n)

    def meta_copy(k):
        to = (me + k) % n
        return copy(meta_ref, meta_buf.at[me], meta_send.at[k], meta_recv.at[me], to)

    @pl.loop(1, n)
    def _(k):
        meta_copy(k).start()

    start_phase(0)

    for u in range(units):
        buf[u, me] = x_ref[u]
    meta_buf[me] = meta_ref[...]
    own = normed_rows(x_ref[...].reshape(units * per * rows, width))
    q_buf[...] = jnp.dot(own, wq_ref[...], preferred_element_type=F32).astype(BF16).reshape(
        units * per, rows, width
    )
    gate_buf[...] = jax.nn.sigmoid(
        jnp.dot(own, wg_ref[...], preferred_element_type=F32)
    ).reshape(units * per, rows, width)
    lane_head = lax.broadcasted_iota(jnp.int32, (heads, rows, width), 2) // head_size
    row_head = lax.broadcasted_iota(jnp.int32, (heads, rows, width), 0)
    mask_buf[...] = (lane_head == row_head).astype(F32).astype(BF16)

    pass_on(0)
    for p in range(1, phases):
        start_phase(p)

    @pl.loop(1, n)
    def _(k):
        j = (me + k) % n
        copy(meta_ref, meta_buf.at[j], meta_send.at[k], meta_recv.at[j], j).wait_recv()

    lanes = meta_ref.shape[1]
    spread_to = (
        lax.broadcasted_iota(jnp.int32, (lanes, keys), 0)
        == lax.broadcasted_iota(jnp.int32, (lanes, keys), 1) % rows
    ).astype(F32)
    tiled = jnp.dot(
        meta_buf[...].reshape(n * 8, lanes), spread_to,
        precision=lax.Precision.HIGHEST, preferred_element_type=F32,
    ).reshape(n, 8, keys)
    owner = lax.broadcasted_iota(jnp.int32, (n, 8, keys), 2) // rows
    block = lax.broadcasted_iota(jnp.int32, (n, 8, keys), 0)
    meta_all = jnp.sum(jnp.where(owner == block, tiled, 0.0), axis=0)
    chain_keys = meta_all[0:1].astype(jnp.int32)
    residue_keys = meta_all[1:2].astype(jnp.int32)
    penalty = (meta_all[2:3] - 1.0) * MASK_PENALTY
    table = rel_ref[...]
    high = table.astype(BF16)
    left = table - high.astype(F32)
    middle = left.astype(BF16)
    low = (left - middle.astype(F32)).astype(BF16)
    table3 = jnp.concatenate([high, middle, low], axis=0)
    bins = lax.broadcasted_iota(jnp.int32, (rel_bins, keys), 0)
    for q in range(rows):
        offset = jnp.clip(residue_ref[q] - residue_keys, -reach, reach) + reach
        bucket = jnp.where(chain_ref[q] == chain_keys, offset, rel_bins - 1)
        hot = (bucket == bins).astype(F32).astype(BF16)
        rel3 = jnp.dot(table3, hot, preferred_element_type=F32)
        rel = rel3[:heads] + rel3[heads : 2 * heads] + rel3[2 * heads :]
        pb = lax.dot_general(wp_ref[...], pair_ref[q], NT, preferred_element_type=F32)
        bias_buf[:, q, :] = pb + rel + penalty

    def attend(u, i):
        s = u * per + i
        x = normed_rows(buf[u, :, i].reshape(keys, width))
        key = jnp.dot(x, wk_ref[...], preferred_element_type=F32).astype(BF16)
        value = jnp.dot(x, wv_ref[...], preferred_element_type=F32).astype(BF16)
        mask = mask_buf[...]
        query = (mask * q_buf[s][None]).reshape(heads * rows, width)
        scores = lax.dot_general(query, key, NT, preferred_element_type=F32) * scale
        scores = scores + bias_buf[...].reshape(heads * rows, keys)
        probs = jnp.exp(scores - jnp.max(scores, axis=-1, keepdims=True))
        mass = jnp.sum(probs, axis=-1, keepdims=True)
        got = jnp.dot(probs.astype(BF16), value, preferred_element_type=F32) * (1.0 / mass)
        got = jnp.sum(got.reshape(heads, rows, width) * mask.astype(F32), axis=0)
        gated_buf[s] = (gate_buf[s] * got).astype(BF16)

    pass_back(0)
    for p in range(phases):
        if p + 1 < phases:
            pass_on(p + 1)
        finish_phase(p)
        if p + 1 < phases:
            attend(2 * p, 0)
            pass_back(p + 1)
            for i in range(1, per):
                attend(2 * p, i)
        else:
            for i in range(per):
                attend(2 * p, i)
        for i in range(per):
            attend(2 * p + 1, i)

    gated = gated_buf[...].reshape(units * per * rows, width)
    out = jnp.dot(gated, wo_ref[...], preferred_element_type=F32)
    out = out.reshape(units, per, rows, width) + x_ref[...].astype(F32)
    out_ref[...] = out.astype(BF16)

    @pl.loop(1, n)
    def _(k):
        meta_copy(k).wait_send()

    for p in range(phases):
        own_across(p).wait_send()
        own_partner(p).wait_send()

        @pl.loop(1, 2 * nz)
        def _(k):
            first_copy(p, k).wait_send()
            forward_across(p, k).wait_send()

            @pl.when(k != 1)
            def _():
                forward_partner(p, k).wait_send()

        @pl.loop(0, 2 * nz)
        def _(k):
            forward_partner_across(p, k).wait_send()


def shards(
    single, pair, chain, residue, valid, w_query, w_key, w_value, w_gate, w_out, w_pair, rel_table
):
    rows, samples, width = single.shape
    n = lax.axis_size("tok")
    ny = 2
    nz = n // (2 * ny)
    units = 4
    per = samples // units
    heads = w_pair.shape[1]
    keys = pair.shape[1]
    x = jnp.transpose(single, (1, 0, 2)).reshape(units, per, rows, width)
    lanes = -(-rows // 128) * 128
    meta = jnp.pad(
        jnp.stack([chain, residue, valid]).astype(F32), ((0, 5), (0, lanes - rows))
    )
    vmem = pl.BlockSpec(memory_space=pltpu.VMEM)
    smem = pl.BlockSpec(memory_space=pltpu.SMEM)
    phases = units // 2
    out = pl.pallas_call(
        functools.partial(kernel, n, ny),
        out_shape=jax.ShapeDtypeStruct(x.shape, BF16),
        in_specs=[vmem, vmem, smem, smem] + [vmem] * 8,
        out_specs=vmem,
        scratch_shapes=[
            pltpu.VMEM((units, n, per, rows, width), BF16),
            pltpu.VMEM((n, 8, lanes), F32),
            pltpu.VMEM((heads, rows, width), BF16),
            pltpu.VMEM((heads, rows, keys), F32),
            pltpu.VMEM((samples, rows, width), BF16),
            pltpu.VMEM((samples, rows, width), F32),
            pltpu.VMEM((samples, rows, width), BF16),
            pltpu.SemaphoreType.DMA((n,)),
            pltpu.SemaphoreType.DMA((n,)),
            pltpu.SemaphoreType.DMA((units, n)),
            pltpu.SemaphoreType.DMA((phases, 2 * nz)),
            pltpu.SemaphoreType.DMA((phases, 2 * nz)),
            pltpu.SemaphoreType.DMA((phases, n)),
        ],
        compiler_params=pltpu.CompilerParams(
            collective_id=0, has_side_effects=True, vmem_limit_bytes=56 * 1024 * 1024
        ),
        cost_estimate=pl.CostEstimate(
            flops=7 * 10**9, bytes_accessed=10**7, transcendentals=10**6
        ),
    )(x, meta, chain, residue, pair, w_query, w_key, w_value, w_gate, w_out, w_pair.T, rel_table.T)
    return jnp.transpose(out.reshape(samples, rows, width), (1, 0, 2))


def solution(mesh):
    split = P(("groups", "tok"))
    rows = P(("groups", "tok"), None, None)
    return jax.shard_map(
        shards,
        mesh=mesh,
        in_specs=(rows, rows, split, split, split) + (P(),) * 7,
        out_specs=rows,
        check_vma=False,
    )
```

time: 110 us -> 49.9 us (0.45)
  the two profiles are of different devices: /device:TPU:0 before, /device:TPU:8 now
where the time goes in v1:
time: 49.9 us; the launch traced here: 49.7 us
  Pallas kernels  45.1 us (90%)
  local copies, waits for them, and re-layouts  3.89 us (8%)
  other arithmetic  0.7 us (1%)
    pallas_call x1, Pallas kernels, shards(): pl.pallas_call(functools.partial(kernel, n, ny), out_shape=jax.ShapeDtype...  45.1 us
    reshape x1, local copies, waits for them, and re-layouts, shards(): return jnp.transpose(out.reshape(samples, rows, width), (1, 0, 2))  1.66 us
    transpose x1, local copies, waits for them, and re-layouts, shards(): x = jnp.transpose(single, (1, 0, 2)).reshape(units, per, rows, width)  1.64 us

profile of v1, /device:TPU:8, one launch (start us, length us, event | category | flops | bytes accessed | tf_op | source)
XLA Modules:
  0.0 49.7 jit_solution(10998880492070645993)
XLA Ops:
  0.0 0.7 %add_convert_fusion = f32[3,16]{1,0:T(4,128)S(1)} fusion(s32[1,16]{1,0:T(1,128)} %bitcast.14, s32[1,16]{1,0:T(1,128)} %bitcast.15, s32[1,16]{1,0:T(1,128)} %bitcast.16), kind=kLoop, calls=%fused_computation.1 | loop fusion | flops 144 | bytes 384 | tf_op jit(solution)/shard_map/convert_element_type | solution.py:274
  0.7 0.6 %pad.4.meta_ref = f32[8,128]{1,0:T(8,128)} pad(f32[3,16]{1,0:T(4,128)S(1)} %add_convert_fusion, f32[]{:T(128)} %constant.2.clone.1), padding=0_5x0_112 | pad | bytes 4292 | tf_op jit(solution)/shard_map/jit(_pad)/pad | solution.py:273
  1.3 1.6 %copy.13 = bf16[8,16,768]{2,1,0:T(8,128)(2,1)} copy(bf16[8,16,768]{2,0,1:T(8,128)(2,1)} %bitcast.11) | data formatting | bytes 393216 | tf_op jit(solution)/shard_map/transpose | solution.py:271
  2.9 45.1 %shard_map.118 = bf16[4,2,16,768]{3,2,1,0:T(8,128)(2,1)} custom-call(bf16[4,2,16,768]{3,2,1,0:T(8,128)(2,1)} %bitcast.13, f32[8,128]{1,0:T(8,128)} %pad.4.meta_ref, s32[16]{0:T(128)} %chain_ref.1, s32[16]{0:T(128)} %residue_ref.1, bf16[16,256,128]{2,1,0:T(8,128)(2,1)} %pair_ref.1, bf16[768,768]{1,0:T(8,128)(2,1)} %wq_ref.1, bf16[768,768]{1,0:T(8,128)(2,1)} %wk_ref.1, ...), custom_call_target="tpu_custom_call" | custom-call | flops 7000000000 | bytes 10000000 | tf_op jit(solution)/shard_map/pallas_call | solution.py:279
  48.0 1.7 %copy.16 = bf16[8,16,768]{2,0,1:T(8,128)(2,1)} copy(bf16[8,16,768]{2,1,0:T(8,128)(2,1)} %bitcast.12) | data formatting | bytes 393216 | tf_op jit(solution)/shard_map/reshape | solution.py:306

commit v2 on v1

v2 whole, which is shorter than its diff:
```python
import functools
import math

import jax
import jax.numpy as jnp
from jax import lax
from jax.experimental import pallas as pl
from jax.experimental.pallas import tpu as pltpu
from jax.sharding import PartitionSpec as P

NORM_EPS = 1e-05
MASK_PENALTY = 10000.0
F32 = jnp.float32
BF16 = jnp.bfloat16
NT = (((1,), (1,)), ((), ()))


def normed_rows(x):
    x = x.astype(F32)
    mean = jnp.mean(x, axis=-1, keepdims=True)
    centred = x - mean
    spread = jnp.mean(centred * centred, axis=-1, keepdims=True)
    return (centred * lax.rsqrt(spread + NORM_EPS)).astype(BF16)


def kernel(
    n, ny, single_ref, chain_row, residue_row, valid_row, chain_ref, residue_ref, wp_ref, rel_ref,
    pair_hbm, wq_hbm, wk_hbm, wv_hbm, wg_hbm, wo_hbm, out_ref,
    buf, x_ref, meta_ref, meta_buf, mask_buf, bias_buf, q_buf, gate_buf, gated_buf, wide_buf,
    pair_ref, wq_ref, wk_ref, wv_ref, wg_ref, wo_ref,
    load, meta_send, meta_recv, recv, send_x, send_up, send_down, send_y, send_c,
):
    units, per, rows, width = x_ref.shape
    heads = wp_ref.shape[0]
    head_size = width // heads
    keys = n * rows
    rel_bins = rel_ref.shape[1]
    reach = (rel_bins - 2) // 2
    scale = 1.0 / math.sqrt(head_size)
    nz = n // (2 * ny)
    phases = units // 2
    me = lax.axis_index("tok")
    c = me % 2
    y = (me // 2) % ny
    z = me // (2 * ny)

    def place(zz, yy, cc):
        return (zz * ny + yy) * 2 + cc

    partner = place(z, y, 1 - c)
    across = place(z, (y + 1) % ny, c)
    above = place((z + 1) % nz, y, c)
    below = place((z + nz - 1) % nz, y, c)
    loads = [
        pltpu.make_async_copy(src, dst, load.at[i])
        for i, (src, dst) in enumerate(
            [
                (wq_hbm, wq_ref), (wg_hbm, wg_ref), (pair_hbm, pair_ref),
                (wk_hbm, wk_ref), (wv_hbm, wv_ref), (wo_hbm, wo_ref),
            ]
        )
    ]
    barrier = pltpu.get_barrier_semaphore()
    for to in (above, below, across, partner):
        pl.semaphore_signal(
            barrier, inc=1, device_id={"tok": to}, device_id_type=pl.DeviceIdType.MESH
        )
    wide_buf[...] = single_ref[...].astype(F32)
    for s in range(units * per):
        x_ref[s // per, s % per] = wide_buf[:, s, :].astype(BF16)
    meta_ref[...] = jnp.zeros_like(meta_ref)
    meta_ref[0:1, 0:rows] = chain_row[...].astype(F32)
    meta_ref[1:2, 0:rows] = residue_row[...].astype(F32)
    meta_ref[2:3, 0:rows] = valid_row[...].astype(F32)
    for u in range(units):
        buf[u, me] = x_ref[u]
    meta_buf[me] = meta_ref[...]
    pl.semaphore_wait(barrier, 4)

    def copy(src, dst, ssem, rsem, to):
        return pltpu.make_async_remote_copy(
            src_ref=src, dst_ref=dst, send_sem=ssem, recv_sem=rsem,
            device_id={"tok": to}, device_id_type=pl.DeviceIdType.MESH,
        )

    def block(u, j, ssem, to):
        return copy(buf.at[u, j], buf.at[u, j], ssem, recv.at[u, j], to)

    def meta_block(j, way, to):
        return copy(meta_buf.at[j], meta_buf.at[j], meta_send.at[way, j], meta_recv.at[j], to)

    def when(cond, fn):
        pl.when(cond)(fn)

    def routes(p, dz, go, cc, act, first):
        zz = z + dz
        j = place(zz, y, cc)
        u = 2 * p + c
        slot = zz * 2 + cc

        def along():
            if go >= 0:
                when(z < nz - 1, lambda: act(block(u, j, send_up.at[p, slot], above)))
            if go <= 0:
                when(z > 0, lambda: act(block(u, j, send_down.at[p, slot], below)))

        along()
        act(block(u, j, send_y.at[p, slot], across))
        if not first:
            act(block(u, j, send_c.at[p, j], partner))

    def meta_routes(dz, go, act):
        j = place(z + dz, y, c)
        if go >= 0:
            when(z < nz - 1, lambda: act(meta_block(j, 0, above)))
        if go <= 0:
            when(z > 0, lambda: act(meta_block(j, 1, below)))
        act(meta_block(j, 2, across))
        act(meta_block(j, 3, partner))

    def start(op):
        op.start()

    def end(op):
        op.wait_send()

    def wait_unit(u, j):
        block(u, j, send_c.at[0, 0], partner).wait_recv()

    def wait_meta(j):
        meta_block(j, 0, partner).wait_recv()

    def own_out(p, act):
        act(block(2 * p + 1 - c, me, send_x.at[p], partner))
        routes(p, 0, 0, c, act, False)

    def partner_out(p, act, wait):
        if wait:
            wait_unit(2 * p + c, partner)
        routes(p, 0, 0, 1 - c, act, True)

    def hop(p, h, act, wait):
        def from_below():
            if p == 0:
                if wait:
                    wait_meta(place(z - h, y, c))
                meta_routes(-h, 1, act)
            for cc in (c, 1 - c):
                if wait:
                    wait_unit(2 * p + c, place(z - h, y, cc))
                routes(p, -h, 1, cc, act, False)

        def from_above():
            if p == 0:
                if wait:
                    wait_meta(place(z + h, y, c))
                meta_routes(h, -1, act)
            for cc in (c, 1 - c):
                if wait:
                    wait_unit(2 * p + c, place(z + h, y, cc))
                routes(p, h, -1, cc, act, False)

        when(z - h >= 0, from_below)
        when(z + h < nz, from_above)

    def back(p, dz, act, wait):
        def go():
            if p == 0:
                j = place(z + dz, (y + 1) % ny, c)
                if wait:
                    wait_meta(j)
                act(meta_block(j, 3, partner))
            for cc in (c, 1 - c):
                j = place(z + dz, (y + 1) % ny, cc)
                if wait:
                    wait_unit(2 * p + c, j)
                act(block(2 * p + c, j, send_c.at[p, j], partner))

        when((z + dz >= 0) & (z + dz < nz), go)

    def backs(p, h, act, wait):
        back(p, h, act, wait)
        back(p, -h, act, wait)

    def hops(p, low, high, act=start, wait=True):
        if high - low <= 4:
            for h in range(low, high):
                hop(p, h, act, wait)
        else:
            pl.loop(low, high)(lambda h: hop(p, h, act, wait))

    def all_backs(p, low, high, act=start, wait=True):
        if high - low <= 4:
            for h in range(low, high):
                backs(p, h, act, wait)
        else:
            pl.loop(low, high)(lambda h: backs(p, h, act, wait))

    def finish_phase(p):
        @pl.loop(1, n)
        def _(k):
            j = (me + k) % n

            @pl.when(j != partner)
            def _():
                wait_unit(2 * p + 1 - c, j)

        wait_unit(2 * p + 1 - c, partner)

    meta_routes(0, 0, start)
    for p in range(phases):
        own_out(p, start)
    for op in loads:
        op.start()
    for p in range(phases):
        partner_out(p, start, True)
    own = normed_rows(x_ref[...].reshape(units * per * rows, width))
    lane_head = lax.broadcasted_iota(jnp.int32, (heads, rows, width), 2) // head_size
    row_head = lax.broadcasted_iota(jnp.int32, (heads, rows, width), 0)
    mask_buf[...] = (lane_head == row_head).astype(F32).astype(BF16)
    loads[0].wait()
    q_buf[...] = jnp.dot(own, wq_ref[...], preferred_element_type=F32).astype(BF16).reshape(
        units * per, rows, width
    )
    hops(0, 1, 2)
    hops(1, 1, 2)
    back(0, 0, start, True)
    loads[1].wait()
    gate_buf[...] = jax.nn.sigmoid(
        jnp.dot(own, wg_ref[...], preferred_element_type=F32)
    ).reshape(units * per, rows, width)
    hops(0, 2, nz)
    back(1, 0, start, True)
    hops(1, 2, min(3, nz))
    all_backs(0, 1, nz)

    @pl.loop(0, nz * ny)
    def _(k):
        wait_meta(k * 2 + 1 - c)

    for op in loads[2:]:
        op.wait()
    lanes = meta_ref.shape[1]
    spread_to = (
        lax.broadcasted_iota(jnp.int32, (lanes, keys), 0)
        == lax.broadcasted_iota(jnp.int32, (lanes, keys), 1) % rows
    ).astype(F32)
    tiled = jnp.dot(
        meta_buf[...].reshape(n * 8, lanes), spread_to,
        precision=lax.Precision.HIGHEST, preferred_element_type=F32,
    ).reshape(n, 8, keys)
    owner = lax.broadcasted_iota(jnp.int32, (n, 8, keys), 2) // rows
    holder = lax.broadcasted_iota(jnp.int32, (n, 8, keys), 0)
    meta_all = jnp.sum(jnp.where(owner == holder, tiled, 0.0), axis=0)
    chain_keys = meta_all[0:1].astype(jnp.int32)
    residue_keys = meta_all[1:2].astype(jnp.int32)
    penalty = (meta_all[2:3] - 1.0) * MASK_PENALTY
    table = rel_ref[...]
    high = table.astype(BF16)
    left = table - high.astype(F32)
    middle = left.astype(BF16)
    low = (left - middle.astype(F32)).astype(BF16)
    table3 = jnp.concatenate([high, middle, low], axis=0)
    bins = lax.broadcasted_iota(jnp.int32, (rel_bins, keys), 0)
    for q in range(rows):
        offset = jnp.clip(residue_ref[q] - residue_keys, -reach, reach) + reach
        bucket = jnp.where(chain_ref[q] == chain_keys, offset, rel_bins - 1)
        hot = (bucket == bins).astype(F32).astype(BF16)
        rel3 = jnp.dot(table3, hot, preferred_element_type=F32)
        rel = rel3[:heads] + rel3[heads : 2 * heads] + rel3[2 * heads :]
        pb = lax.dot_general(wp_ref[...], pair_ref[q], NT, preferred_element_type=F32)
        bias_buf[:, q, :] = pb + rel + penalty

    def attend(u, i):
        s = u * per + i
        x = normed_rows(buf[u, :, i].reshape(keys, width))
        key = jnp.dot(x, wk_ref[...], preferred_element_type=F32).astype(BF16)
        value = jnp.dot(x, wv_ref[...], preferred_element_type=F32).astype(BF16)
        mask = mask_buf[...]
        query = (mask * q_buf[s][None]).reshape(heads * rows, width)
        scores = lax.dot_general(query, key, NT, preferred_element_type=F32) * scale
        scores = scores + bias_buf[...].reshape(heads * rows, keys)
        probs = jnp.exp(scores - jnp.max(scores, axis=-1, keepdims=True))
        mass = jnp.sum(probs, axis=-1, keepdims=True)
        got = jnp.dot(probs.astype(BF16), value, preferred_element_type=F32) * (1.0 / mass)
        got = jnp.sum(got.reshape(heads, rows, width) * mask.astype(F32), axis=0)
        gated_buf[s] = (gate_buf[s] * got).astype(BF16)

    hops(1, min(3, nz), nz)
    finish_phase(0)
    attend(0, 0)
    all_backs(1, 1, nz)
    for i in range(1, per):
        attend(0, i)
    for i in range(per):
        attend(1, i)
    for p in range(1, phases):
        finish_phase(p)
        for i in range(per):
            attend(2 * p, i)
        for i in range(per):
            attend(2 * p + 1, i)

    gated = gated_buf[...].reshape(units * per * rows, width)
    out = jnp.dot(gated, wo_ref[...], preferred_element_type=F32)
    out = out.reshape(units * per, rows, width)
    for s in range(units * per):
        wide_buf[:, s, :] = wide_buf[:, s, :] + out[s]
    out_ref[...] = wide_buf[...].astype(BF16)

    meta_routes(0, 0, end)
    for p in range(phases):
        own_out(p, end)
        partner_out(p, end, False)
        hops(p, 1, nz, end, False)
        back(p, 0, end, False)
        all_backs(p, 1, nz, end, False)


def shards(
    single, pair, chain, residue, valid, w_query, w_key, w_value, w_gate, w_out, w_pair, rel_table
):
    rows, samples, width = single.shape
    n = lax.axis_size("tok")
    ny = 2
    nz = n // (2 * ny)
    units = 4
    per = samples // units
    heads = w_pair.shape[1]
    keys = pair.shape[1]
    lanes = -(-rows // 128) * 128
    vmem = pl.BlockSpec(memory_space=pltpu.VMEM)
    smem = pl.BlockSpec(memory_space=pltpu.SMEM)
    hbm = pl.BlockSpec(memory_space=pl.ANY)
    phases = units // 2
    weight = pltpu.VMEM(w_query.shape, BF16)
    dma = pltpu.SemaphoreType.DMA
    return pl.pallas_call(
        functools.partial(kernel, n, ny),
        out_shape=jax.ShapeDtypeStruct(single.shape, BF16),
        in_specs=[vmem] * 4 + [smem] * 2 + [vmem] * 2 + [hbm] * 6,
        out_specs=vmem,
        scratch_shapes=[
            pltpu.VMEM((units, n, per, rows, width), BF16),
            pltpu.VMEM((units, per, rows, width), BF16),
            pltpu.VMEM((8, lanes), F32),
            pltpu.VMEM((n, 8, lanes), F32),
            pltpu.VMEM((heads, rows, width), BF16),
            pltpu.VMEM((heads, rows, keys), F32),
            pltpu.VMEM((samples, rows, width), BF16),
            pltpu.VMEM((samples, rows, width), F32),
            pltpu.VMEM((samples, rows, width), BF16),
            pltpu.VMEM((rows, samples, width), F32),
            pltpu.VMEM(pair.shape, BF16),
            weight, weight, weight, weight, weight,
            dma((6,)),
            dma((4, n)),
            dma((n,)),
            dma((units, n)),
            dma((phases,)),
            dma((phases, 2 * nz)),
            dma((phases, 2 * nz)),
            dma((phases, 2 * nz)),
            dma((phases, n)),
        ],
        compiler_params=pltpu.CompilerParams(
            collective_id=0, has_side_effects=True, vmem_limit_bytes=56 * 1024 * 1024
        ),
        cost_estimate=pl.CostEstimate(
            flops=7 * 10**9, bytes_accessed=10**7, transcendentals=10**6
        ),
    )(
        single, chain.reshape(1, rows), residue.reshape(1, rows), valid.reshape(1, rows),
        chain, residue, w_pair.T, rel_table.T, pair, w_query, w_key, w_value, w_gate, w_out,
    )


def solution(mesh):
    split = P(("groups", "tok"))
    rows = P(("groups", "tok"), None, None)
    return jax.shard_map(
        shards,
        mesh=mesh,
        in_specs=(rows, rows, split, split, split) + (P(),) * 7,
        out_specs=rows,
        check_vma=False,
    )
```

time: 49.9 us -> 40.3 us (0.81)
  the two profiles are of different devices: /device:TPU:8 before, /device:TPU:0 now
where the time goes in v2:
time: 40.3 us; the launch traced here: 40.1 us
  Pallas kernels  38.5 us (96%)
  local copies, waits for them, and re-layouts  1.62 us (4%)
    pallas_call x1, Pallas kernels, shards(): pl.pallas_call(functools.partial(kernel, n, ny), out_shape=jax.ShapeDtype...  38.5 us
    unnamed x1, local copies, waits for them, and re-layouts  1.62 us

profile of v2, /device:TPU:0, one launch (start us, length us, event | category | flops | bytes accessed | tf_op | source)
XLA Modules:
  0.0 40.1 jit_solution(14162664143316462809)
XLA Ops:
  0.0 38.5 %shard_map.118 = bf16[16,8,768]{2,1,0:T(8,128)(2,1)} custom-call(bf16[16,8,768]{2,1,0:T(8,128)(2,1)} %single_ref.1, s32[1,16]{1,0:T(1,128)} %bitcast.7, s32[1,16]{1,0:T(1,128)} %bitcast.8, s32[1,16]{1,0:T(1,128)} %bitcast.9, s32[16]{0:T(128)} %chain_ref.1, s32[16]{0:T(128)} %residue_ref.1, bf16[16,128]{1,0:T(8,128)(2,1)} %bitcast.6, f32[16,66]{1,0:T(8,128)} %bitcast.5, ...), custom_call_target="tpu_custom_call" | custom-call | flops 7000000000 | bytes 10000000 | tf_op jit(solution)/shard_map/pallas_call | solution.py:338
  38.5 1.6 %copy.14 = bf16[16,8,768]{2,1,0:T(8,128)(2,1)} copy(bf16[16,8,768]{2,1,0:T(8,128)(2,1)} %shard_map.118) | data formatting | bytes 393216

commit v3 on v2

--- a/solution.py
+++ b/solution.py
@@ -229,9 +229,11 @@
     gate_buf[...] = jax.nn.sigmoid(
         jnp.dot(own, wg_ref[...], preferred_element_type=F32)
     ).reshape(units * per, rows, width)
-    hops(0, 2, nz)
+    hops(0, 2, min(3, nz))
+    hops(1, 2, min(3, nz))
     back(1, 0, start, True)
-    hops(1, 2, min(3, nz))
+    hops(0, min(3, nz), nz)
+    hops(1, min(3, nz), nz)
     all_backs(0, 1, nz)
 
     @pl.loop(0, nz * ny)
@@ -286,7 +288,6 @@
         got = jnp.sum(got.reshape(heads, rows, width) * mask.astype(F32), axis=0)
         gated_buf[s] = (gate_buf[s] * got).astype(BF16)
 
-    hops(1, min(3, nz), nz)
     finish_phase(0)
     attend(0, 0)
     all_backs(1, 1, nz)

time: 40.3 us -> 39.9 us (0.990)
  no operation moved by 1% of the time
where the time goes in v3:
time: 39.9 us; the launch traced here: 39.7 us
  Pallas kernels  38.1 us (95%)
  local copies, waits for them, and re-layouts  1.62 us (4%)
    pallas_call x1, Pallas kernels, shards(): pl.pallas_call(functools.partial(kernel, n, ny), out_shape=jax.ShapeDtype...  38.1 us
    unnamed x1, local copies, waits for them, and re-layouts  1.62 us

profile of v3, /device:TPU:0, one launch (start us, length us, event | category | flops | bytes accessed | tf_op | source)
XLA Modules:
  0.0 39.7 jit_solution(4773733441468181857)
XLA Ops:
  0.0 38.1 %shard_map.118 = bf16[16,8,768]{2,1,0:T(8,128)(2,1)} custom-call(bf16[16,8,768]{2,1,0:T(8,128)(2,1)} %single_ref.1, s32[1,16]{1,0:T(1,128)} %bitcast.7, s32[1,16]{1,0:T(1,128)} %bitcast.8, s32[1,16]{1,0:T(1,128)} %bitcast.9, s32[16]{0:T(128)} %chain_ref.1, s32[16]{0:T(128)} %residue_ref.1, bf16[16,128]{1,0:T(8,128)(2,1)} %bitcast.6, f32[16,66]{1,0:T(8,128)} %bitcast.5, ...), custom_call_target="tpu_custom_call" | custom-call | flops 7000000000 | bytes 10000000 | tf_op jit(solution)/shard_map/pallas_call | solution.py:339
  38.1 1.6 %copy.14 = bf16[16,8,768]{2,1,0:T(8,128)(2,1)} copy(bf16[16,8,768]{2,1,0:T(8,128)(2,1)} %shard_map.118) | data formatting | bytes 393216
